TPU v7x, 256 devices: a whole 4x4x8 slice. The times are simulated.
256 devices in a mesh: row: 8 (over y, z_hi), col: 32 (over x, z_lo, core).
Axes of the slice: x: 4, y: 4, z: 8 (z_hi: 2, z_lo: 4; z = z_hi * 4 + z_lo), core: 2. Of those that a mesh axis runs over, the one named last changes fastest.
Arguments:
- matrix: bfloat16 [16384, 16384], P('row', 'col'), may hold values from 0 to 250, as said below
- pivots: int32 [512], replicated, may hold values from 0 to 16383, as said below
- lower_inverse: bfloat16 [512, 512], replicated, may hold values from 0 to 250, as said below
- upper_inverse: bfloat16 [512, 512], replicated, may hold values from 0 to 250, as said below
Outputs:
- factored: float32 [16384, 16384], P('row', 'col')
Inputs may be any that keep to these rules, and one draw needn't show every extreme that they name: The entries are distinct; pivots[j] is either j or a row of 512 to 16383. `matrix`: integers 0 to 250. `lower_inverse`: integers 0 to 250, unit lower triangular. `upper_inverse`: integers 0 to 250, upper triangular with diagonal 1 to 250.
All inputs are finite; a program needn't handle non-finite values.
Results may differ from a plain program's by a relative error of at most 0.0003.
Values may be sent and summed in bfloat16 or wider, within the bound.
A program may use at most 64 MiB of HBM per device.

v0:
```python
import jax
import jax.numpy as jnp
from jax import lax
from jax.sharding import PartitionSpec as P

DEPTH = 128


def spread(array, axis, root):
    mine = lax.axis_index(axis) == root
    return lax.psum(jnp.where(mine, array, jnp.zeros_like(array)), axis)


def reduce_mod(x):
    quot = jnp.floor(x * (1.0 / 251.0))
    rest = x - quot * 251.0
    rest = jnp.where(rest < 0, rest + 251.0, rest)
    return jnp.where(rest >= 251.0, rest - 251.0, rest)


def product_mod(left, right):
    steps = left.shape[1] // DEPTH
    total = jnp.zeros((left.shape[0], right.shape[1]), jnp.float32)
    for step in range(steps):
        part = jnp.dot(
            left[:, step * DEPTH : (step + 1) * DEPTH],
            right[step * DEPTH : (step + 1) * DEPTH],
            preferred_element_type=jnp.float32,
        )
        total = total + reduce_mod(part)
    return reduce_mod(total)


def per_device(matrix, pivots, lower_inverse, upper_inverse):
    rows_dev, cols_dev = matrix.shape
    panel = lower_inverse.shape[0]
    row_pos = lax.axis_index("row")
    col_pos = lax.axis_index("col")
    owner = pivots // rows_dev
    local = pivots % rows_dev
    mine = owner == row_pos
    zeros_rows = jnp.zeros((panel, cols_dev), jnp.bfloat16)
    picked = jnp.where(mine[:, None], matrix[jnp.clip(local, 0, rows_dev - 1)], zeros_rows)
    new_top = lax.psum(picked, "row").astype(jnp.float32).astype(jnp.bfloat16)
    old_top = spread(matrix[:panel], "row", 0)
    moving = mine & (pivots != jnp.arange(panel, dtype=jnp.int32))
    target = jnp.where(moving, local, rows_dev)
    swapped = matrix.at[target].set(old_top, mode="drop")
    swapped = swapped.at[:panel].set(jnp.where(row_pos == 0, new_top, swapped[:panel]))
    upper_block = product_mod(lower_inverse, new_top).astype(jnp.bfloat16)
    lower_local = product_mod(swapped, upper_inverse).astype(jnp.bfloat16)
    lower_block = spread(lower_local, "col", 0)
    swapped_wide = swapped.astype(jnp.float32)
    trailing = reduce_mod(swapped_wide - product_mod(lower_block, upper_block))
    right_part = trailing.at[:panel].set(
        jnp.where(row_pos == 0, upper_block.astype(jnp.float32), trailing[:panel])
    )
    global_rows = row_pos * rows_dev + jnp.arange(rows_dev, dtype=jnp.int32)
    left_part = jnp.where(
        (global_rows < panel)[:, None], swapped_wide, lower_block.astype(jnp.float32)
    )
    result = right_part.at[:, :panel].set(jnp.where(col_pos == 0, left_part, right_part))
    return result / 251.0


def solution(mesh):
    placed = (P("row", "col"), P(), P(), P())
    return jax.shard_map(
        per_device, mesh=mesh, in_specs=placed, out_specs=P("row", "col"), check_vma=False
    )
```

profile of v0, /device:TPU:41, one launch (start us, length us, event | category | flops | bytes accessed | tf_op | source)
XLA Modules:
  0.0 460.5 jit_solution(1964169761772329911)
XLA Ops:
  6.5 0.0 copy-start.3
  6.5 0.0 all-reduce.6.cloned.1.call-start
  6.5 1.6 copy.20
  8.1 0.0 copy-done.3
  8.2 2.0 gather_fusion
  10.2 1.1 slice_select_fusion.2
  11.3 0.0 all-reduce.6.cloned.1.call-update
  11.3 0.0 all-reduce.4.cloned.1.call-start
  11.4 131.1 %all-reduce.6.cloned.1.call-done = (bf16[512,512]{1,0:T(8,128)(2,1)}, bf16[512,512]{1,0:T(8,128)(2,1)}) async-done(((bf16[512,512]{1,0:T(8,128)(2,1)}, bf16[512,512]{1,0:T(8,128)(2,1)}), (bf16[512,512]{1,0:T(8,128)(2,1)}, bf16[512,512]{1,0:T(8,128)(2,1)})) %all-reduce.6.cloned.1.call-update) | async-done | bytes 1048592 | tf_op jit(solution)/shard_map/psum | solution.py:11
  142.5 0.0 copy-start.1
  142.5 0.0 copy-start.2
  142.5 4.0 scatter_fusion
  146.5 0.0 copy-done.1
  146.6 0.2 fusion.28
  146.8 0.0 copy-done.2
  146.8 0.7 fusion.22
  147.5 0.7 fusion.24
  148.2 0.7 fusion.26
  148.9 8.7 %broadcast_select_fusion = bf16[2048,512]{1,0:T(8,128)(2,1)} fusion(pred[]{:T(512)S(6)} %eq.17, f32[2048,512]{1,0:T(8,128)S(1)} %fusion.22, f32[2048,512]{1,0:T(8,128)S(1)} %fusion.24, f32[2048,512]{1,0:T(8,128)S(1)} %fusion.26, bf16[2048,512]{1,0:T(8,128)(2,1)S(1)} %fusion.28, bf16[512,512]{1,0:T(8,128)(2,1)S(1)} %copy-done.2), kind=kOutput, calls=%fused_computation.45 | convolution fusion | flops 326107136 | bytes 15335425 | tf_op jit(solution)/shard_map/dot_general | solution.py:25
  157.6 0.0 all-reduce.4.cloned.1.call-update
  157.6 1.2 convolution_bitcast_fusion.1
  158.8 1.2 convolution_bitcast_fusion.2
  160.0 1.2 convolution_bitcast_fusion.3
  161.2 3.1 fusion.12
  164.3 274.4 %all-reduce.4.cloned.1.call-done = bf16[2048,512]{1,0:T(8,128)(2,1)} async-done(((bf16[2048,512]{1,0:T(8,128)(2,1)}), bf16[2048,512]{1,0:T(8,128)(2,1)}) %all-reduce.4.cloned.1.call-update) | async-done | bytes 2097168 | tf_op jit(solution)/shard_map/psum | solution.py:11
  438.7 0.0 copy-start
  438.7 1.9 fusion.19
  440.6 0.0 copy-done
  440.6 0.7 fusion.17
  441.3 0.7 fusion.15
  442.0 8.9 %compare_select_fusion = f32[2048,512]{1,0:T(8,128)S(1)} fusion(bf16[2048,512]{1,0:T(8,128)(2,1)S(1)} %fusion.28, f32[2048,512]{1,0:T(8,128)S(1)} %fusion.15, f32[2048,512]{1,0:T(8,128)S(1)} %fusion.17, f32[2048,512]{1,0:T(8,128)S(1)} %fusion.19, bf16[2048,512]{1,0:T(8,128)(2,1)S(1)} %copy-done, bf16[512,512]{1,0:T(8,128)(2,1)S(1)} %fusion.12), kind=kOutput, calls=%fused_computation.2 | convolution fusion | flops 336592896 | bytes 19529728 | tf_op jit(solution)/shard_map/dot_general | solution.py:25
  450.9 0.3 fusion.13
  451.2 2.5 fusion.1
  (3 shorter events, 0.0 us)
Async XLA Ops:
  6.5 1.6 copy-start.3
  6.5 136.0 %all-reduce.6.cloned.1.call-start = ((), (), s32[]{:S(2)}) async-start(), calls=%async_computation.1 | async-start | bytes 2097152 | tf_op jit(solution)/shard_map/psum | solution.py:11
  11.3 427.4 %all-reduce.4.cloned.1.call-start = ((), (), s32[]{:S(2)}) async-start(), calls=%async_computation | async-start | bytes 4194304 | tf_op jit(solution)/shard_map/psum | solution.py:11
  142.5 4.1 copy-start.1
  142.5 4.3 copy-start.2
  438.7 1.9 copy-start
Sparse Core Ops, SparseCore 0:
  11.4 131.0 all-reduce.5
  157.7 280.9 all-reduce.3
where the time goes:
time: 467 us; the launch traced here: 461 us
  waiting for transfers between devices  406 us (87%)
  matrix products  29.5 us (6%)
  between operations  13.5 us (3%)
  local copies, waits for them, and re-layouts  7.63 us (2%)
    psum x2, waiting for transfers between devices, spread(): return lax.psum(jnp.where(mine, array, jnp.zeros_like(array)), axis)  406 us
    dot_general x12, matrix products, product_mod(): jnp.dot(left[:, step * DEPTH:(step + 1) * DEPTH], right[step * DEPTH:(ste...  29.5 us
  transfers between devices with their start and end apart: 2, of which 2 were waited for; matrix products, arithmetic and copies ran while one was open for 1% of the time, Pallas kernels for 0%

commit v1 on v0

v1 whole, which is shorter than its diff:
```python
import functools

import jax
import jax.numpy as jnp
from jax import lax
from jax.experimental import pallas as pl
from jax.experimental.pallas import tpu as pltpu
from jax.sharding import PartitionSpec as P

MESH = pl.DeviceIdType.MESH
PRIME = 251.0
INVERSE = 1.0 / 251.0
NY, NX, NZ = 4, 4, 4


def residue(x):
    rest = x - jnp.floor(x * INVERSE + 0.5) * PRIME
    return jnp.where(rest < 0, rest + PRIME, rest)


def balanced(x):
    return x - jnp.floor(x * INVERSE + 0.5) * PRIME


def dot(a, b):
    return jnp.dot(a, b, preferred_element_type=jnp.float32)


def exchange_kernel(
    piv_ref, s_ref, pf, cf, tt, xf, pcol, oh, g, r1, zs, r2, msg,
    raw_send, raw_recv, cor_send, cor_recv, src_send, row_send, row_recv, loc,
):
    rows = s_ref.shape[0]
    panel = xf.shape[0]
    piece = rows // (NX * NZ)
    small = panel // (NX * NZ)
    part = panel // NY
    r = lax.axis_index("row")
    c = lax.axis_index("col")
    y, h = r // 2, r % 2
    x, z, k = c // 8, (c // 2) % 4, c % 2
    me = x * NZ + z

    def chip(x2, z2, k2=0):
        return {"row": r, "col": x2 * 8 + z2 * 2 + k2}

    def along(y2, h2):
        return {"row": y2 * 2 + h2, "col": c}

    def signal(device):
        pl.semaphore_signal(barrier, 1, device_id=device, device_id_type=MESH)

    barrier = pltpu.get_barrier_semaphore()
    for step in range(1, 8):
        signal({"row": (r + step) % 8, "col": c})
    signal(chip(x, z, 1 - k))

    @pl.when(k == 0)
    def _():
        for step in range(1, NX * NZ):
            other = (me + step) % (NX * NZ)
            signal(chip(other // NZ, other % NZ))

    @pl.when(k == 0)
    def _():
        pl.semaphore_wait(barrier, 7 + NX * NZ)

    @pl.when(k == 1)
    def _():
        pl.semaphore_wait(barrier, 8)

    def remote(src, dst, send, recv, device):
        return pltpu.make_async_remote_copy(
            src_ref=src, dst_ref=dst, send_sem=send, recv_sem=recv,
            device_id=device, device_id_type=MESH,
        )

    def raw(p, slot, device, source=None):
        ref = pf if source is None else source
        return remote(
            ref.at[pl.ds(p * piece, piece)], pf.at[pl.ds(p * piece, piece)],
            raw_send.at[slot], raw_recv.at[p], device,
        )

    def cor(p, slot, device, source=None):
        ref = cf if source is None else source
        return remote(
            ref.at[pl.ds(p * small, small)], cf.at[pl.ds(p * small, small)],
            cor_send.at[slot], cor_recv.at[p], device,
        )

    is_core = k == 0
    is_src = (k == 0) & (me == 0)
    is_first = is_src & (r == 0)
    own_copy = pltpu.make_async_copy(s_ref, pf, loc.at[0])
    cor_copy = pltpu.make_async_copy(s_ref.at[pl.ds(0, small)], cf.at[pl.ds(0, small)], loc.at[1])

    def first_cor(p):
        return remote(
            s_ref.at[pl.ds(p * small, small)], cf.at[pl.ds(p * small, small)],
            src_send.at[16 + p], cor_recv.at[p], chip(p // NZ, p % NZ),
        )

    def first_raw(p):
        return remote(
            s_ref.at[pl.ds(p * piece, piece)], pf.at[pl.ds(p * piece, piece)],
            src_send.at[p], raw_recv.at[p], chip(p // NZ, p % NZ),
        )

    def core_raw(p):
        return remote(
            pf.at[pl.ds(p * piece, piece)], pf.at[pl.ds(p * piece, piece)],
            src_send.at[32 + p], raw_recv.at[p], chip(x, z, 1),
        )

    def core_src(p):
        return remote(
            s_ref.at[pl.ds(p * piece, piece)], pf.at[pl.ds(p * piece, piece)],
            src_send.at[32 + p], raw_recv.at[p], chip(x, z, 1),
        )

    core_cor = remote(cf, cf, src_send.at[48], loc.at[2], chip(x, z, 1))
    order = (8, 4, 12, 1, 9, 5, 13, 2, 10, 6, 14, 3, 11, 7, 15)

    @pl.when(is_first)
    def _():
        cor_copy.start()
        for p in order:
            first_cor(p).start()

    @pl.when(is_src)
    def _():
        for p in order:
            first_raw(p).start()
        own_copy.start()
        for p in range(16):
            core_src(p).start()

    lane = lax.broadcasted_iota(jnp.int32, (panel, 128), 1)
    for t in range(panel // 128):
        line = jnp.broadcast_to(piv_ref[:, t * 128 : (t + 1) * 128], (128, 128))
        pcol[t * 128 : (t + 1) * 128, :] = jnp.transpose(line)
    named = pcol[...]

    def build(t, carry):
        hit = named == lane + (r * rows + t * 128)
        oh[:, pl.ds(pl.multiple_of(t * 128, 128), 128)] = jnp.where(hit, 1.0, 0.0).astype(jnp.bfloat16)
        return carry

    lax.fori_loop(0, rows // 128, build, 0)

    def owner_of(start, size):
        return pcol[pl.ds(start, size), :] // rows

    def wide(mask_value, width):
        return jnp.concatenate([mask_value] * (width // 128), axis=1)

    def pick(t, carry):
        start = pl.multiple_of(t * 256, 256)
        picked = dot(oh[pl.ds(start, 256), :], s_ref[...])
        owner = wide(owner_of(start, 256), panel)
        old = s_ref[pl.ds(start, 256), :].astype(jnp.float32)
        use = (owner * jnp.where(r == 0, 1, 0)) == 0
        g[pl.ds(start, 256), :] = jnp.where(use, picked, old).astype(jnp.bfloat16)
        return carry

    lax.fori_loop(0, panel // 256, pick, 0)

    def one(d):
        y2 = (y + d) % NY
        return remote(
            g.at[pl.ds(pl.multiple_of(y2 * part, part), part)], r1.at[d - 1],
            row_send.at[d - 1], row_recv.at[d - 1], along(y2, h),
        )

    def two():
        return remote(zs, r2, row_send.at[3], row_recv.at[3], along(y, 1 - h))

    def three(d):
        return remote(
            msg.at[d - 1], xf.at[pl.ds(pl.multiple_of(y * part, part), part)],
            row_send.at[3 + d], row_recv.at[3 + d], along((y + d) % NY, h),
        )

    def three_in(d):
        return remote(
            msg.at[d - 1], xf.at[pl.ds(pl.multiple_of(((y + NY - d) % NY) * part, part), part)],
            row_send.at[3 + d], row_recv.at[3 + d], along((y + d) % NY, h),
        )

    for d in (2, 1, 3):
        one(d).start()

    def spread_raw_x(p, slot):
        for step in range(1, NX):
            raw(p, slot + step - 1, chip((x + step) % NX, z)).start()

    def spread_cor_x(p, slot):
        for step in range(1, NX):
            cor(p, slot + step - 1, chip((x + step) % NX, z)).start()

    @pl.when(is_core & (me != 0))
    def _():
        raw(me, 0, chip(x, z)).wait_recv()
        for step in range(1, NZ):
            z2 = (z + step) % NZ

            @pl.when((x > 0) | (z2 > 0))
            def _():
                raw(me, step - 1, chip(x, z2)).start()

        for step in range(1, NX):
            x2 = (x + step) % NX

            @pl.when((z > 0) | (x2 > 0))
            def _():
                raw(me, 2 + step, chip(x2, z)).start()

        @pl.when(x == 0)
        def _():
            for step in range(1, NX):
                raw(me, 14 + step, chip(step, 0)).start()

        core_raw(me).start()

    @pl.when(is_src)
    def _():
        for step in range(1, NZ):
            raw(0, step - 1, chip(0, step), s_ref).start()
        for step in range(1, NX):
            raw(0, 2 + step, chip(step, 0), s_ref).start()

    def own_cor():
        for step in range(1, NZ):
            cor(me, step - 1, chip(x, (z + step) % NZ)).start()
        spread_cor_x(me, 3)

    def down(step):
        return remote(
            cf.at[pl.ds(me * small, small)], cf.at[pl.ds(me * small, small)],
            cor_send.at[14 + step], cor_recv.at[me], {"row": step, "col": c},
        )

    @pl.when(is_first)
    def _():
        cor_copy.wait()

    @pl.when(is_core & (r == 0) & (me != 0))
    def _():
        cor(me, 0, chip(x, z)).wait_recv()

    @pl.when(is_core & (r == 0))
    def _():
        for step in range(1, 8):
            down(step).start()
        own_cor()

    def halves():
        home = pl.ds(pl.multiple_of(y * part, part), part)
        owner = wide(owner_of(pl.multiple_of(y * part, part), part), panel)
        first = jnp.zeros((part, panel), jnp.float32)
        rest = jnp.zeros((part, panel), jnp.float32)
        for d in range(NY):
            got = (g[home, :] if d == 0 else r1[d - 1]).astype(jnp.float32)
            flag = jnp.where(((y + NY - d) % NY == 0) & (h == 0), 1.0, 0.0)
            first = first + got * flag
            rest = rest + got * (1.0 - flag)
        return owner, first, rest

    for d in (1, 3, 2):
        one(d).wait_recv()
    owner, first, rest = halves()
    low = jnp.where(h == 0, 1, 0)
    away = (owner % 2 == 0) & (owner != 0)
    zs[...] = jnp.where(away | (owner * low != owner), rest, jnp.where(low == 1, first, rest)).astype(jnp.bfloat16)
    two().start()

    @pl.when(is_core & (me != 0))
    def _():
        for step in range(1, NZ):
            z2 = (z + step) % NZ
            p = x * NZ + z2
            raw(p, 0, chip(x, z)).wait_recv()
            for leap in range(1, NX):
                x2 = (x + leap) % NX

                @pl.when((z > 0) | (x2 > 0))
                def _():
                    raw(p, 3 + 3 * step + leap - 1, chip(x2, z)).start()

            core_raw(p).start()

    @pl.when(is_core & (r != 0))
    def _():
        cor(me, 0, chip(x, z)).wait_recv()
        own_cor()

    @pl.when(is_core)
    def _():
        for step in range(1, NZ):
            p = x * NZ + (z + step) % NZ
            cor(p, 0, chip(x, z)).wait_recv()
            spread_cor_x(p, 3 + 3 * step)

    two().wait_recv()
    owner, first, rest = halves()
    got = r2[...].astype(jnp.float32)
    odd = owner % 2 == 1
    low_t = jnp.where(odd, got, jnp.where(owner == 0, first, rest))
    high_t = jnp.where(odd, rest, got)
    flag = jnp.where(h == 0, 1.0, 0.0)
    new = low_t * flag + high_t * (1.0 - flag)
    old = first * flag + got * (1.0 - flag)
    for d in (2, 1, 3):
        y2 = (y + d) % NY
        msg[d - 1] = jnp.where(owner == y2 * 2 + h, old, new).astype(jnp.bfloat16)
        three(d).start()
    xf[pl.ds(pl.multiple_of(y * part, part), part), :] = jnp.where(owner == r, old, new).astype(jnp.bfloat16)

    @pl.when(is_core & (me != 0))
    def _():
        for leap in range(1, NX):
            x2 = (x + leap) % NX
            for z2 in range(NZ):
                p = x2 * NZ + z2
                raw(p, 0, chip(x, z)).wait_recv()
                core_raw(p).start()

    @pl.when(is_core)
    def _():
        for leap in range(1, NX):
            x2 = (x + leap) % NX
            for z2 in range(NZ):
                cor(x2 * NZ + z2, 0, chip(x, z)).wait_recv()
        core_cor.start()

    for d in (1, 3, 2):
        three_in(d).wait_recv()

    def finish(t, carry):
        start = pl.multiple_of(t * 128, 128)
        owner = wide(owner_of(start, 128), panel)
        mine = g[pl.ds(start, 128), :].astype(jnp.float32)
        got = xf[pl.ds(start, 128), :].astype(jnp.float32)
        tt[pl.ds(start, 128), :] = jnp.where(owner == r, mine, got).astype(jnp.bfloat16)
        return carry

    lax.fori_loop(0, panel // 128, finish, 0)

    @pl.when(r == 0)
    def _():
        xf[...] = s_ref[0:panel, :]

    for d in (1, 2, 3):
        one(d).wait_send()
        three(d).wait_send()
    two().wait_send()

    @pl.when(k == 1)
    def _():
        for p in range(16):
            raw(p, 0, chip(x, z)).wait_recv()
        core_cor.wait_recv()

    @pl.when(is_src)
    def _():
        own_copy.wait()
        for p in order:
            first_raw(p).wait_send()
        for p in range(16):
            core_src(p).wait_send()
        for slot in range(6):
            raw(0, slot, chip(x, z)).wait_send()

    @pl.when(is_first)
    def _():
        for p in order:
            first_cor(p).wait_send()

    @pl.when(is_core & (r == 0))
    def _():
        for step in range(1, 8):
            down(step).wait_send()

    @pl.when(is_core)
    def _():
        for slot in range(15):
            cor(0, slot, chip(x, z)).wait_send()
        core_cor.wait_send()

    @pl.when(is_core & (me != 0))
    def _():
        for step in range(1, NZ):
            @pl.when((x > 0) | ((z + step) % NZ > 0))
            def _():
                raw(0, step - 1, chip(x, z)).wait_send()

        for step in range(4):
            for leap in range(1, NX):
                @pl.when((z > 0) | ((x + leap) % NX > 0))
                def _():
                    raw(0, 3 + 3 * step + leap - 1, chip(x, z)).wait_send()

        @pl.when(x == 0)
        def _():
            for step in range(1, NX):
                raw(0, 14 + step, chip(x, z)).wait_send()

        for p in range(16):
            core_raw(p).wait_send()


def exchange(piv, s, panel):
    rows, cols = s.shape
    part = panel // NY
    bf = jnp.bfloat16
    dma = pltpu.SemaphoreType.DMA
    vmem = pl.BlockSpec(memory_space=pltpu.VMEM)
    return pl.pallas_call(
        exchange_kernel,
        out_shape=[
            jax.ShapeDtypeStruct((rows, panel), bf),
            jax.ShapeDtypeStruct((panel, panel), bf),
            jax.ShapeDtypeStruct((panel, cols), bf),
            jax.ShapeDtypeStruct((panel, cols), bf),
        ],
        in_specs=[vmem, vmem],
        out_specs=[vmem] * 4,
        scratch_shapes=[
            pltpu.VMEM((panel, 128), jnp.int32),
            pltpu.VMEM((panel, rows), bf),
            pltpu.VMEM((panel, cols), bf),
            pltpu.VMEM((NY - 1, part, cols), bf),
            pltpu.VMEM((part, cols), bf),
            pltpu.VMEM((part, cols), bf),
            pltpu.VMEM((NY - 1, part, cols), bf),
            dma((18,)), dma((16,)), dma((22,)), dma((16,)), dma((49,)), dma((7,)), dma((7,)), dma((3,)),
        ],
        compiler_params=pltpu.CompilerParams(
            collective_id=0, has_side_effects=True, vmem_limit_bytes=48 << 20
        ),
        name="exchange",
    )(piv, s)


def update_kernel(piv_ref, s_ref, p_ref, cf, tt, xf, linv, uinv, o_ref, w, rep, top):
    tile = s_ref.shape[0]
    panel = w.shape[0]
    step = pl.program_id(0)
    r = lax.axis_index("row")
    c = lax.axis_index("col")
    bf = jnp.bfloat16
    left = jnp.where(c == 0, 1.0, 0.0)

    @pl.when(step == 0)
    def _():
        ub = balanced(uinv[...].astype(jnp.float32)).astype(bf)
        lb = balanced(linv[...].astype(jnp.float32)).astype(bf)
        new = tt[...]
        both = balanced(dot(ub, lb)).astype(bf)
        right = balanced(dot(both, new))
        w[...] = jnp.where(c == 0, -ub.astype(jnp.float32), right).astype(bf)
        old = jnp.where(c == 0, 0.0, xf[...].astype(jnp.float32))
        rep[...] = (residue(old - dot(cf[...], w[...])) + 1.0).astype(bf)

        @pl.when(r == 0)
        def _():
            upper = residue(dot(lb, new))
            top[...] = jnp.where(c == 0, new.astype(jnp.float32), upper) * INVERSE

    rows = lax.broadcasted_iota(jnp.int32, (tile, panel), 0) + (
        r * (tile * pl.num_programs(0)) + step * tile
    )
    hit = jnp.where(rows == piv_ref[...], 1.0, 0.0).astype(bf)
    swapped = dot(hit, rep[...])
    raw = jnp.where(c == 0, 0.0, s_ref[...].astype(jnp.float32))
    rest = residue(raw - dot(p_ref[...], w[...]))
    o_ref[...] = jnp.where(swapped > 0, swapped - 1.0, rest) * INVERSE

    @pl.when((r == 0) & (step * tile < panel))
    def _():
        o_ref[...] = top[pl.ds(pl.multiple_of(step * tile, tile), tile), :]


def update(piv, s, pf, cf, tt, xf, linv, uinv):
    rows, cols = s.shape
    panel = cf.shape[0]
    tile = 256
    whole = lambda shape: pl.BlockSpec(shape, lambda i: (0, 0))
    tiled = pl.BlockSpec((tile, cols), lambda i: (i, 0))
    square = whole((panel, panel))
    return pl.pallas_call(
        update_kernel,
        grid=(rows // tile,),
        out_shape=jax.ShapeDtypeStruct((rows, cols), jnp.float32),
        in_specs=[whole((1, panel)), tiled, pl.BlockSpec((tile, panel), lambda i: (i, 0))] + [square] * 5,
        out_specs=tiled,
        scratch_shapes=[
            pltpu.VMEM((panel, cols), jnp.bfloat16),
            pltpu.VMEM((panel, cols), jnp.bfloat16),
            pltpu.VMEM((panel, cols), jnp.float32),
        ],
        compiler_params=pltpu.CompilerParams(vmem_limit_bytes=48 << 20),
        name="update",
    )(piv, s, pf, cf, tt, xf, linv, uinv)


def per_device(matrix, pivots, lower_inverse, upper_inverse):
    panel = lower_inverse.shape[0]
    piv = pivots.reshape(1, panel)
    pf, cf, tt, xf = exchange(piv, matrix, panel)
    return update(piv, matrix, pf, cf, tt, xf, lower_inverse, upper_inverse)


def solution(mesh):
    placed = (P("row", "col"), P(), P(), P())
    return jax.shard_map(
        per_device, mesh=mesh, in_specs=placed, out_specs=P("row", "col"), check_vma=False
    )
```

time: 467 us -> 75.6 us (0.16)
  the two profiles are of different devices: /device:TPU:41 before, /device:TPU:67 now
where the time goes in v1:
time: 75.6 us; the launch traced here: 75.3 us
  Pallas kernels  71.7 us (95%)
  local copies, waits for them, and re-layouts  3.61 us (5%)
    pallas_call x1, Pallas kernels, exchange(): pl.pallas_call(exchange_kernel, out_shape=[jax.ShapeDtypeStruct((rows, pa...  60.9 us
    pallas_call x1, Pallas kernels, update(): pl.pallas_call(update_kernel, grid=(rows // tile,), out_shape=jax.ShapeDt...  10.8 us
    unnamed x10, local copies, waits for them, and re-layouts  3.61 us

profile of v1, /device:TPU:67, one launch (start us, length us, event | category | flops | bytes accessed | tf_op | source)
XLA Modules:
  0.0 75.3 jit_solution(10394190471630315690)
XLA Ops:
  0.0 0.0 copy-start
  0.0 1.6 %copy-done = bf16[2048,512]{1,0:T(8,128)(2,1)S(1)} copy-done((bf16[2048,512]{1,0:T(8,128)(2,1)S(1)}, bf16[2048,512]{1,0:T(8,128)(2,1)}, u32[]{:S(2)}) %copy-start) | copy-done | bytes 2097176
  1.6 0.0 copy-start.4
  1.6 0.7 copy-done.4
  2.3 0.0 copy-start.2
  2.3 0.0 copy-start.3
  2.3 60.9 %exchange.1 = (bf16[2048,512]{1,0:T(8,128)(2,1)S(1)}, bf16[512,512]{1,0:T(8,128)(2,1)S(1)}, bf16[512,512]{1,0:T(8,128)(2,1)S(1)}, bf16[512,512]{1,0:T(8,128)(2,1)S(1)}) custom-call(s32[1,512]{1,0:T(1,128)S(1)} %bitcast.1, bf16[2048,512]{1,0:T(8,128)(2,1)S(1)} %copy-done), custom_call_target="tpu_custom_call" | custom-call | tf_op jit(solution)/shard_map/exchange/pallas_call | solution.py:419
  63.2 0.0 copy-start.1
  63.2 1.3 %copy-done.1 = bf16[2048,512]{1,0:T(8,128)(2,1)} copy-done((bf16[2048,512]{1,0:T(8,128)(2,1)}, bf16[2048,512]{1,0:T(8,128)(2,1)S(1)}, u32[]{:S(2)}) %copy-start.1) | copy-done | bytes 2097176
  64.6 0.0 copy-done.2
  64.6 0.0 copy-done.3
  64.6 10.8 %update.1 = f32[2048,512]{1,0:T(8,128)} custom-call(s32[1,512]{1,0:T(1,128)S(1)} %bitcast.2, bf16[2048,512]{1,0:T(8,128)(2,1)S(1)} %copy-done, bf16[2048,512]{1,0:T(8,128)(2,1)} %copy-done.1, bf16[512,512]{1,0:T(8,128)(2,1)S(1)} %get-tuple-element.10.cf, bf16[512,512]{1,0:T(8,128)(2,1)S(1)} %get-tuple-element.11.tt, ...), custom_call_target="tpu_custom_call" | custom-call | tf_op jit(solution)/shard_map/update/pallas_call | solution.py:492
Async XLA Ops:
  0.0 1.6 %copy-start = (bf16[2048,512]{1,0:T(8,128)(2,1)S(1)}, bf16[2048,512]{1,0:T(8,128)(2,1)}, u32[]{:S(2)}) copy-start(bf16[2048,512]{1,0:T(8,128)(2,1)} %s_ref.3) | copy-start | bytes 6291460
  1.6 0.7 copy-start.4
  2.3 62.3 %copy-start.2 = (bf16[512,512]{1,0:T(8,128)(2,1)S(1)}, bf16[512,512]{1,0:T(8,128)(2,1)}, u32[]{:S(2)}) copy-start(bf16[512,512]{1,0:T(8,128)(2,1)} %linv.1) | copy-start | bytes 1572868
  2.3 62.3 %copy-start.3 = (bf16[512,512]{1,0:T(8,128)(2,1)S(1)}, bf16[512,512]{1,0:T(8,128)(2,1)}, u32[]{:S(2)}) copy-start(bf16[512,512]{1,0:T(8,128)(2,1)} %uinv.1) | copy-start | bytes 1572868
  63.2 1.3 %copy-start.1 = (bf16[2048,512]{1,0:T(8,128)(2,1)}, bf16[2048,512]{1,0:T(8,128)(2,1)S(1)}, u32[]{:S(2)}) copy-start(bf16[2048,512]{1,0:T(8,128)(2,1)S(1)} %get-tuple-element.9.p_ref) | copy-start | bytes 6291460

commit v2 on v0

v2 whole, which is shorter than its diff:
```python
import functools

import jax
import jax.numpy as jnp
from jax import lax
from jax.experimental import pallas as pl
from jax.experimental.pallas import tpu as pltpu
from jax.sharding import PartitionSpec as P

MESH = pl.DeviceIdType.MESH
PRIME = 251.0
INVERSE = 1.0 / 251.0
ROUND = 1.5 * 2.0**23
NY, NX, NZ = 4, 4, 4
CHUNKS = 2
FIX = 4


def balanced(x):
    quot = (x * INVERSE + ROUND) - ROUND
    return x - quot * PRIME


def residue(x):
    rest = balanced(x)
    return jnp.where(rest < 0, rest + PRIME, rest)


def dot(a, b):
    return jnp.dot(a, b, preferred_element_type=jnp.float32)


def exchange_kernel(
    piv_hbm, linv_hbm, uinv_hbm, s_hbm, o_hbm, piv_ref, linv, uinv, out, pf, tt, xf, both, wk, rep, s_ref, pcol, oh, g, r1, zs, r2, msg,
    net_send, net_recv, src_send, src_recv, core_send, core_recv, down_send, row_send, row_recv, loc, out_sem,
):
    rows = s_ref.shape[0]
    panel = xf.shape[0]
    half = rows // 2
    line = half // NX
    piece = line // 4
    fix = panel // 2
    part = panel // NY
    r = lax.axis_index("row")
    c = lax.axis_index("col")
    y, h = r // 2, r % 2
    x, z, k = c // 8, (c // 2) % 4, c % 2
    first_plane = z == 0
    is_src = first_plane & (x == 0)
    loads = [
        pltpu.make_async_copy(src, dst, loc.at[2 + i])
        for i, (src, dst) in enumerate(
            ((piv_hbm, piv_ref), (s_hbm, s_ref), (uinv_hbm, uinv), (linv_hbm, linv))
        )
    ]
    for load in loads:
        load.start()

    def chip(x2, z2):
        return {"row": r, "col": x2 * 8 + z2 * 2 + k}

    def along(y2, h2):
        return {"row": y2 * 2 + h2, "col": c}

    sibling = {"row": r, "col": c + 1 - 2 * k}
    barrier = pltpu.get_barrier_semaphore()

    def signal(device):
        pl.semaphore_signal(barrier, 1, device_id=device, device_id_type=MESH)

    signal(sibling)
    for step in range(1, 4):
        signal(chip((x + step) % NX, z))
        signal(chip(x, (z + step) % NZ))
    for step in range(1, 8):
        signal({"row": (r + step) % 8, "col": c})

    def remote(src, dst, send, recv, device):
        return pltpu.make_async_remote_copy(
            src_ref=src, dst_ref=dst, send_sem=send, recv_sem=recv,
            device_id=device, device_id_type=MESH,
        )

    def place(q, t):
        if isinstance(t, int) and t == FIX:
            return pl.ds(pl.multiple_of(rows + k * fix + q * piece, piece), piece)
        return pl.ds(pl.multiple_of(k * half + t * line + q * piece, piece), piece)

    def net(q, t, slot, device):
        return remote(
            pf.at[place(q, t)], pf.at[place(q, t)], net_send.at[slot], net_recv.at[q * 5 + t], device
        )

    def arrived(q, t):
        net(q, t, 0, sibling).wait_recv()

    def sent(slot):
        net(0, 0, slot, sibling).wait_send()

    def src_piece(ref, q, t, slot, device):
        return remote(
            ref.at[place(q, t)], pf.at[place(q, t)], src_send.at[slot], net_recv.at[q * 5 + t], device
        )

    def line_place(k2, q):
        return pl.ds(pl.multiple_of(k2 * half + q * line, line), line)

    def core_line(q):
        return remote(
            pf.at[line_place(k, q)], pf.at[line_place(k, q)], core_send.at[q], core_recv.at[q], sibling
        )

    def core_line_in(q):
        return remote(
            pf.at[line_place(1 - k, q)], pf.at[line_place(1 - k, q)],
            core_send.at[q], core_recv.at[q], sibling,
        )

    def fix_place(k2):
        return pl.ds(pl.multiple_of(rows + k2 * fix, fix), fix)

    def core_fix():
        return remote(
            pf.at[fix_place(k)], pf.at[fix_place(k)], core_send.at[4], core_recv.at[4], sibling
        )

    def core_fix_in():
        return remote(
            pf.at[fix_place(1 - k)], pf.at[fix_place(1 - k)],
            core_send.at[4], core_recv.at[4], sibling,
        )

    def give(k2, q):
        at = pl.ds(k2 * half + q * line, line)
        return remote(
            s_hbm.at[at], pf.at[at], src_send.at[16 + k2 * 4 + q],
            src_recv.at[q] if k2 else core_recv.at[q], sibling,
        )

    def give_fix():
        return remote(
            s_hbm.at[pl.ds(fix, fix)], pf.at[pl.ds(rows + fix, fix)],
            src_send.at[24], src_recv.at[4], sibling,
        )

    own_copy = pltpu.make_async_copy(s_hbm, pf.at[pl.ds(0, rows)], loc.at[0])
    own_fix = pltpu.make_async_copy(s_hbm.at[pl.ds(0, fix)], pf.at[pl.ds(rows, fix)], loc.at[1])

    def fix_out(q, slot):
        return remote(
            pf.at[place(q, 4)], pf.at[place(q, 4)], src_send.at[slot], net_recv.at[q * 5 + 4], chip(q, 0)
        )

    def down(step):
        return remote(
            pf.at[place(x, FIX)], pf.at[place(x, FIX)], down_send.at[step // 2 if isinstance(step, int) else 0],
            net_recv.at[x * 5 + FIX], {"row": step, "col": c},
        )

    plan = (
        (2, 0, 2, 0), (3, 0, 3, 0), (0, 0, 0, 1), (1, 0, 1, 0), (2, 2, 3, 0), (0, 1, 0, 1),
        (2, 1, 2, 0), (3, 1, 3, 0), (1, 1, 1, 0), (2, 3, 3, 0), (0, 2, 0, 1),
        (1, 2, 1, 0), (3, 2, 3, 0), (0, 3, 0, 1), (1, 3, 1, 0), (3, 3, 3, 0),
    )

    def fix_sends():
        for q in (2, 1, 3):
            fix_out(q, 25 + q).start()
        for step in (1, 2, 4, 6):
            down(step).start()

    @pl.when(is_src)
    def _():
        pl.semaphore_wait(barrier, 14)

        @pl.when(k == 0)
        def _():
            @pl.when(r == 0)
            def _():
                give_fix().start()
                own_fix.start()

            for q in (0, 2, 1, 3):
                give(1, q).start()

            @pl.when(r == 0)
            def _():
                own_fix.wait()
                fix_sends()

            for slot, (q, t, x2, z2) in enumerate(plan):
                src_piece(s_hbm, q, t, slot, chip(x2, z2)).start()

            own_copy.start()
            for q in range(4):
                give(0, q).start()

        @pl.when(k == 1)
        def _():
            @pl.when(r == 0)
            def _():
                remote(
                    pf.at[fix_place(1)], pf.at[fix_place(1)], src_send.at[24], src_recv.at[4], sibling
                ).wait_recv()
                fix_sends()

            ready = []
            for slot, (q, t, x2, z2) in enumerate(plan):
                if t not in ready:
                    ready.append(t)
                    remote(
                        pf.at[line_place(1, t)], pf.at[line_place(1, t)],
                        src_send.at[16 + t], src_recv.at[t], sibling,
                    ).wait_recv()
                src_piece(pf, q, t, slot, chip(x2, z2)).start()

    loads[0].wait()
    lane = lax.broadcasted_iota(jnp.int32, (panel, 128), 1)
    for t in range(panel // 128):
        wide_line = jnp.broadcast_to(piv_ref[:, t * 128 : (t + 1) * 128], (128, 128))
        pcol[t * 128 : (t + 1) * 128, :] = jnp.transpose(wide_line)
    named = pcol[...]

    def build(t, carry):
        hit = named == lane + (r * rows + t * 128)
        oh[:, pl.ds(pl.multiple_of(t * 128, 128), 128)] = jnp.where(hit, 1.0, 0.0).astype(jnp.bfloat16)
        return carry

    lax.fori_loop(0, rows // 128, build, 0)

    def owner_of(start, size):
        return pcol[pl.ds(start, size), :] // rows

    def wide(mask_value, width):
        return jnp.concatenate([mask_value] * (width // 128), axis=1)

    width = s_ref.shape[1] // CHUNKS

    def columns(ch):
        return pl.ds(ch * width, width)

    def pick(ch):
        def body(t, carry):
            start = pl.multiple_of(t * 256, 256)
            picked = dot(oh[pl.ds(start, 256), :], s_ref[:, columns(ch)])
            owner = wide(owner_of(start, 256), width)
            old = s_ref[pl.ds(start, 256), columns(ch)].astype(jnp.float32)
            use = (owner * jnp.where(r == 0, 1, 0)) == 0
            g[pl.ds(start, 256), columns(ch)] = jnp.where(use, picked, old).astype(jnp.bfloat16)
            return carry

        lax.fori_loop(0, panel // 256, body, 0)

    def one(d, ch):
        y2 = (y + d) % NY
        return remote(
            g.at[pl.ds(pl.multiple_of(y2 * part, part), part), columns(ch)], r1.at[d - 1, :, columns(ch)],
            row_send.at[7 * ch + d - 1], row_recv.at[7 * ch + d - 1], along(y2, h),
        )

    def two(ch):
        return remote(
            zs.at[:, columns(ch)], r2.at[:, columns(ch)],
            row_send.at[7 * ch + 3], row_recv.at[7 * ch + 3], along(y, 1 - h),
        )

    def three(d, ch):
        return remote(
            msg.at[d - 1, :, columns(ch)], xf.at[pl.ds(pl.multiple_of(y * part, part), part), columns(ch)],
            row_send.at[7 * ch + 3 + d], row_recv.at[7 * ch + 3 + d], along((y + d) % NY, h),
        )

    def three_in(d, ch):
        return remote(
            msg.at[d - 1, :, columns(ch)],
            xf.at[pl.ds(pl.multiple_of(((y + NY - d) % NY) * part, part), part), columns(ch)],
            row_send.at[7 * ch + 3 + d], row_recv.at[7 * ch + 3 + d], along((y + d) % NY, h),
        )

    loads[1].wait()
    pick(0)

    @pl.when(jnp.logical_not(is_src))
    def _():
        pl.semaphore_wait(barrier, 14)

    for ch in range(CHUNKS):
        if ch:
            pick(ch)
        for d in (2, 1, 3):
            one(d, ch).start()

    def goes_x(leap, t):
        if leap == 1:
            return (z > 0) | (x == 1) | ((x == 2) & (t < 2))
        if leap == 3:
            return (z > 0) | (x == 2) | (x == 3)
        return z > 0

    def own(t, carry):
        arrived(x, t)

        @pl.when(first_plane & (x == 3) & (t < 2))
        def _():
            arrived(2, t + 2)
            net(2, t + 2, 38 + t, chip(2, 0)).start()

        @pl.when(z < NZ - 1)
        def _():
            net(x, t, t, chip(x, z + 1)).start()

        for leap in (2, 1, 3):
            @pl.when(goes_x(leap, t))
            def _():
                net(x, t, 5 * leap + t, chip((x + leap) % NX, z)).start()

        return carry

    def own_line(low, high):
        @pl.when(jnp.logical_not(is_src))
        def _():
            lax.fori_loop(low, high, own, 0)

    def own_fix_line():
        arrived(x, FIX)

        @pl.when(first_plane & (h == 0))
        def _():
            down(r + 1).start()

        @pl.when(first_plane)
        def _():
            for step in (3, 2, 1):
                net(x, FIX, (4, 40, 41)[step - 1], chip(x, step)).start()

        for leap in (2, 1, 3):
            net(x, FIX, 5 * leap + FIX, chip((x + leap) % NX, z)).start()

    def goes_back(q):
        return (z == 1) & (((x > 0) & (q == 0)) | ((x == 1) & (q == 3)) | ((x == 3) & (q == 1)))

    def relayed(q, t):
        return first_plane & (x == 3) & (q == 2) & (t >= 2)

    def others(t, carry):
        for leap in (2, 1, 3):
            q = (x + leap) % NX

            @pl.when(jnp.logical_not(relayed(q, t)))
            def _():
                arrived(q, t)

            @pl.when(goes_back(q))
            def _():
                net(q, t, 15 + 5 * leap + t, chip(x, 0)).start()

        return carry

    def other_lines(low, high):
        lax.fori_loop(low, high, others, 0)

    @pl.when(first_plane & (x > 0) & (r == 0))
    def _():
        arrived(x, FIX)
        for step in (1, 2, 4, 6):
            down(step).start()

    own_line(0, jnp.where(z == 0, 4, jnp.where(z == 1, 1, 0)))

    @pl.when(first_plane & (r > 0))
    def _():
        own_fix_line()

    home = pl.ds(pl.multiple_of(y * part, part), part)
    home_owner = wide(owner_of(pl.multiple_of(y * part, part), part), width)

    def halves(ch):
        first = jnp.zeros((part, width), jnp.float32)
        rest = jnp.zeros((part, width), jnp.float32)
        for d in range(NY):
            got = (g[home, columns(ch)] if d == 0 else r1[d - 1, :, columns(ch)]).astype(jnp.float32)
            flag = jnp.where(((y + NY - d) % NY == 0) & (h == 0), 1.0, 0.0)
            first = first + got * flag
            rest = rest + got * (1.0 - flag)
        return first, rest

    low = jnp.where(h == 0, 1, 0)
    for ch in range(CHUNKS):
        for d in (1, 3, 2):
            one(d, ch).wait_recv()
        first, rest = halves(ch)
        away = (home_owner % 2 == 0) & (home_owner != 0)
        sent_rows = jnp.where(away | (home_owner * low != home_owner), rest, jnp.where(low == 1, first, rest))
        zs[:, columns(ch)] = sent_rows.astype(jnp.bfloat16)
        two(ch).start()

    for load in loads[2:]:
        load.wait()

    def inverses():
        ub = balanced(uinv[...].astype(jnp.float32)).astype(jnp.bfloat16)
        lb = balanced(linv[...].astype(jnp.float32)).astype(jnp.bfloat16)
        both[...] = balanced(dot(ub, lb)).astype(jnp.bfloat16)

    pl.when(z != 1)(inverses)

    own_line(
        jnp.where(z == 0, 4, jnp.where(z == 1, 1, 0)),
        jnp.where(z < 3, 4, 2),
    )

    @pl.when(z == 1)
    def _():
        pl.when(r > 0)(own_fix_line)
        other_lines(0, 2)
        core_line(0).start()
        core_line(1).start()

    for ch in range(CHUNKS):
        two(ch).wait_recv()
        first, rest = halves(ch)
        got = r2[:, columns(ch)].astype(jnp.float32)
        odd = home_owner % 2 == 1
        low_t = jnp.where(odd, got, jnp.where(home_owner == 0, first, rest))
        high_t = jnp.where(odd, rest, got)
        flag = jnp.where(h == 0, 1.0, 0.0)
        new = low_t * flag + high_t * (1.0 - flag)
        old = first * flag + got * (1.0 - flag)
        for d in (2, 1, 3):
            y2 = (y + d) % NY
            msg[d - 1, :, columns(ch)] = jnp.where(home_owner == y2 * 2 + h, old, new).astype(jnp.bfloat16)
            three(d, ch).start()
        xf[home, columns(ch)] = jnp.where(home_owner == r, old, new).astype(jnp.bfloat16)

    own_line(jnp.where(z < 3, 4, 2), 4)

    @pl.when((z >= 2) & (r > 0))
    def _():
        own_fix_line()

    @pl.when(z == 1)
    def _():
        other_lines(2, 4)
        core_line(2).start()
        core_line(3).start()
        inverses()

    @pl.when(r > 0)
    def _():
        for leap in (2, 1, 3):
            arrived((x + leap) % NX, FIX)
        core_fix().start()

    bf = jnp.bfloat16
    keep = jnp.where(c == 0, 0.0, 1.0)
    left = balanced(uinv[...].astype(jnp.float32))
    for ch in range(CHUNKS):
        for d in (1, 3, 2):
            three_in(d, ch).wait_recv()

        def finish(t, carry):
            start = pl.multiple_of(t * 128, 128)
            owner = wide(owner_of(start, 128), width)
            mine = g[pl.ds(start, 128), columns(ch)].astype(jnp.float32)
            got = xf[pl.ds(start, 128), columns(ch)].astype(jnp.float32)
            tt[pl.ds(start, 128), columns(ch)] = jnp.where(owner == r, mine, got).astype(bf)
            return carry

        lax.fori_loop(0, panel // 128, finish, 0)
        right = -balanced(dot(both[...], tt[:, columns(ch)]))
        wk[:, columns(ch)] = jnp.where(c == 0, left[:, ch * width : (ch + 1) * width], right).astype(bf)

    @pl.when(r == 0)
    def _():
        xf[...] = s_ref[0:panel, :]
        lb = balanced(linv[...].astype(jnp.float32)).astype(bf)
        upper = residue(dot(lb, tt[...]))
        out[0:panel, :] = jnp.where(c == 0, tt[...].astype(jnp.float32), upper).astype(bf)

    def swapped_in(start):
        old = xf[...].astype(jnp.float32) * keep
        rep[:, 0:panel] = residue(old + dot(pf[start : start + panel, :], wk[...])).astype(bf)
        rep[:, panel : panel + 128] = jnp.ones((panel, 128), bf)

    @pl.when(r > 0)
    def _():
        core_fix_in().wait_recv()
        swapped_in(rows)

    def write(start):
        at = pl.ds(pl.multiple_of(start, panel), panel)
        return pltpu.make_async_copy(out.at[at], o_hbm.at[at], out_sem.at[start // panel])

    def tile(start):
        at = pl.ds(pl.multiple_of(start, panel), panel)

        @pl.when((r > 0) | (start >= panel))
        def _():
            index = lax.broadcasted_iota(jnp.int32, (panel, panel), 0) + (r * rows + start)
            hit = jnp.where(index == piv_ref[...], 1.0, 0.0).astype(bf)
            swapped = dot(hit, rep[...])
            count = wide(swapped[:, panel : panel + 128], panel)
            rest = residue(s_ref[at, :].astype(jnp.float32) * keep + dot(pf[at, :], wk[...]))
            out[at, :] = jnp.where(count > 0, swapped[:, 0:panel], rest).astype(bf)

        write(start).start()

    @pl.when(is_src & (k == 0))
    def _():
        own_copy.wait()

    for i in range(2):
        @pl.when((z != 1) & jnp.logical_not(is_src))
        def _():
            other_lines(2 * i, 2 * i + 2)
            core_line(2 * i).start()
            core_line(2 * i + 1).start()

        def incoming():
            core_line_in(2 * i).wait_recv()
            core_line_in(2 * i + 1).wait_recv()

        from_sibling = jnp.logical_not(is_src & (k == 0))
        if i == 0:
            @pl.when(r == 0)
            def _():
                pl.when(k == 1)(incoming)
                swapped_in(0)

            from_sibling = from_sibling & ((r > 0) | (k == 0))

        def tiles(j, carry):
            @pl.when((j == 1) & from_sibling)
            def _():
                incoming()

            tile(jnp.where(j == 0, k, 1 - k) * half + i * panel)
            return carry

        lax.fori_loop(0, 2, tiles, 0)

    for t in range(4):
        write(t * panel).wait()

    for ch in range(CHUNKS):
        for d in (1, 2, 3):
            one(d, ch).wait_send()
            three(d, ch).wait_send()
        two(ch).wait_send()
    pl.when(r > 0)(lambda: core_fix().wait_send())

    @pl.when(jnp.logical_not(is_src))
    def _():
        for q in range(4):
            core_line(q).wait_send()

        def own_sent(t, carry):
            pl.when(z < NZ - 1)(lambda: sent(t))
            for leap in range(1, 4):
                pl.when(goes_x(leap, t))(lambda: sent(5 * leap + t))
            return carry

        lax.fori_loop(0, 4, own_sent, 0)

    @pl.when(first_plane & (r > 0))
    def _():
        for slot in (4, 40, 41):
            sent(slot)

    for leap in range(1, 4):
        pl.when(r > 0)(lambda: sent(5 * leap + FIX))

        @pl.when(goes_back((x + leap) % NX))
        def _():
            for t in range(4):
                sent(15 + 5 * leap + t)

    @pl.when(first_plane & (x == 3))
    def _():
        sent(38)
        sent(39)

    @pl.when(is_src)
    def _():
        for slot, (q, t, x2, z2) in enumerate(plan):
            src_piece(pf, q, t, slot, chip(x2, z2)).wait_send()

        @pl.when(r == 0)
        def _():
            for q in (2, 1, 3):
                fix_out(q, 25 + q).wait_send()

        @pl.when(k == 0)
        def _():
            for q in range(4):
                give(1, q).wait_send()
                give(0, q).wait_send()

            @pl.when(r == 0)
            def _():
                give_fix().wait_send()

    @pl.when(first_plane & (r == 0))
    def _():
        for step in (1, 2, 4, 6):
            down(step).wait_send()

    @pl.when(first_plane & (r > 0) & (h == 0))
    def _():
        down(r + 1).wait_send()


def step_kernel(piv, linv, uinv, s, panel):
    rows, cols = s.shape
    part = panel // NY
    bf = jnp.bfloat16
    dma = pltpu.SemaphoreType.DMA
    anywhere = pl.BlockSpec(memory_space=pl.ANY)
    return pl.pallas_call(
        exchange_kernel,
        out_shape=jax.ShapeDtypeStruct((rows, cols), bf),
        in_specs=[pl.BlockSpec(memory_space=pltpu.HBM)] * 4,
        out_specs=anywhere,
        scratch_shapes=[
            pltpu.VMEM((1, panel), jnp.int32),
            pltpu.VMEM((panel, panel), bf),
            pltpu.VMEM((panel, panel), bf),
            pltpu.VMEM((rows, cols), bf),
            pltpu.VMEM((rows + panel, panel), bf),
            pltpu.VMEM((panel, cols), bf),
            pltpu.VMEM((panel, cols), bf),
            pltpu.VMEM((panel, panel), bf),
            pltpu.VMEM((panel, cols), bf),
            pltpu.VMEM((panel, cols + 128), bf),
            pltpu.VMEM((rows, cols), bf),
            pltpu.VMEM((panel, 128), jnp.int32),
            pltpu.VMEM((panel, rows), bf),
            pltpu.VMEM((panel, cols), bf),
            pltpu.VMEM((NY - 1, part, cols), bf),
            pltpu.VMEM((part, cols), bf),
            pltpu.VMEM((part, cols), bf),
            pltpu.VMEM((NY - 1, part, cols), bf),
            dma((42,)), dma((20,)), dma((29,)), dma((5,)), dma((5,)), dma((5,)),
            dma((7,)), dma((7 * CHUNKS,)), dma((7 * CHUNKS,)), dma((6,)), dma((4,)),
        ],
        compiler_params=pltpu.CompilerParams(
            collective_id=0, has_side_effects=True, vmem_limit_bytes=60 << 20
        ),
        name="exchange",
    )(piv, linv, uinv, s)


def per_device(matrix, pivots, lower_inverse, upper_inverse):
    panel = lower_inverse.shape[0]
    piv = pivots.reshape(1, panel)
    rest = step_kernel(piv, lower_inverse, upper_inverse, matrix, panel)
    return rest.astype(jnp.float32) * INVERSE


def solution(mesh):
    placed = (P("row", "col"), P(), P(), P())
    return jax.shard_map(
        per_device, mesh=mesh, in_specs=placed, out_specs=P("row", "col"), check_vma=False
    )
```

time: 467 us -> 60.6 us (0.13)
  the two profiles are of different devices: /device:TPU:41 before, /device:TPU:105 now
where the time goes in v2:
time: 60.6 us; the launch traced here: 60.5 us
  Pallas kernels  56.3 us (93%)
  other arithmetic  4.23 us (7%)
    pallas_call x1, Pallas kernels, step_kernel(): pl.pallas_call(exchange_kernel, out_shape=jax.ShapeDtypeStruct((rows, col...  56.3 us
    mul x1, other arithmetic, per_device(): return rest.astype(jnp.float32) * INVERSE  4.23 us

profile of v2, /device:TPU:105, one launch (start us, length us, event | category | flops | bytes accessed | tf_op | source)
XLA Modules:
  0.0 60.5 jit_solution(552295579080043673)
XLA Ops:
  0.0 56.3 %exchange.1 = bf16[2048,512]{1,0:T(8,128)(2,1)} custom-call(s32[1,512]{1,0:T(1,128)} %bitcast.1, bf16[512,512]{1,0:T(8,128)(2,1)} %linv_hbm.1, bf16[512,512]{1,0:T(8,128)(2,1)} %uinv_hbm.1, bf16[2048,512]{1,0:T(8,128)(2,1)} %s_hbm.1), custom_call_target="tpu_custom_call" | custom-call | tf_op jit(solution)/shard_map/exchange/pallas_call | solution.py:619
  56.3 4.2 %convert_multiply_fusion = f32[2048,512]{1,0:T(8,128)} fusion(bf16[2048,512]{1,0:T(8,128)(2,1)} %exchange.1), kind=kLoop, calls=%fused_computation | loop fusion | flops 2097152 | bytes 6291456 | tf_op jit(solution)/shard_map/mul | solution.py:657

commit v3 on v2

--- a/solution.py
+++ b/solution.py
@@ -47,11 +47,13 @@
     x, z, k = c // 8, (c // 2) % 4, c % 2
     first_plane = z == 0
     is_src = first_plane & (x == 0)
+    quarter = rows // 4
+    spans = [pl.ds(i * quarter, quarter) for i in range(4)]
+    pairs = [(piv_hbm, piv_ref)]
+    pairs += [(s_hbm.at[at], s_ref.at[at]) for at in spans]
+    pairs += [(uinv_hbm, uinv), (linv_hbm, linv)]
     loads = [
-        pltpu.make_async_copy(src, dst, loc.at[2 + i])
-        for i, (src, dst) in enumerate(
-            ((piv_hbm, piv_ref), (s_hbm, s_ref), (uinv_hbm, uinv), (linv_hbm, linv))
-        )
+        pltpu.make_async_copy(src, dst, loc.at[2 + i]) for i, (src, dst) in enumerate(pairs)
     ]
     for load in loads:
         load.start()
@@ -133,14 +135,14 @@
     def give(k2, q):
         at = pl.ds(k2 * half + q * line, line)
         return remote(
-            s_hbm.at[at], pf.at[at], src_send.at[16 + k2 * 4 + q],
+            s_hbm.at[at], pf.at[at], src_send.at[28 + k2 * 4 + q],
             src_recv.at[q] if k2 else core_recv.at[q], sibling,
         )
 
     def give_fix():
         return remote(
             s_hbm.at[pl.ds(fix, fix)], pf.at[pl.ds(rows + fix, fix)],
-            src_send.at[24], src_recv.at[4], sibling,
+            src_send.at[36], src_recv.at[4], sibling,
         )
 
     own_copy = pltpu.make_async_copy(s_hbm, pf.at[pl.ds(0, rows)], loc.at[0])
@@ -161,11 +163,11 @@
         (2, 0, 2, 0), (3, 0, 3, 0), (0, 0, 0, 1), (1, 0, 1, 0), (2, 2, 3, 0), (0, 1, 0, 1),
         (2, 1, 2, 0), (3, 1, 3, 0), (1, 1, 1, 0), (2, 3, 3, 0), (0, 2, 0, 1),
         (1, 2, 1, 0), (3, 2, 3, 0), (0, 3, 0, 1), (1, 3, 1, 0), (3, 3, 3, 0),
-    )
+    ) + tuple((0, t, x2, 0) for t in range(4) for x2 in (1, 3, 2))
 
     def fix_sends():
         for q in (2, 1, 3):
-            fix_out(q, 25 + q).start()
+            fix_out(q, 36 + q).start()
         for step in (1, 2, 4, 6):
             down(step).start()
 
@@ -200,7 +202,7 @@
             @pl.when(r == 0)
             def _():
                 remote(
-                    pf.at[fix_place(1)], pf.at[fix_place(1)], src_send.at[24], src_recv.at[4], sibling
+                    pf.at[fix_place(1)], pf.at[fix_place(1)], src_send.at[36], src_recv.at[4], sibling
                 ).wait_recv()
                 fix_sends()
 
@@ -210,7 +212,7 @@
                     ready.append(t)
                     remote(
                         pf.at[line_place(1, t)], pf.at[line_place(1, t)],
-                        src_send.at[16 + t], src_recv.at[t], sibling,
+                        src_send.at[28 + t], src_recv.at[t], sibling,
                     ).wait_recv()
                 src_piece(pf, q, t, slot, chip(x2, z2)).start()
 
@@ -277,7 +279,8 @@
             row_send.at[7 * ch + 3 + d], row_recv.at[7 * ch + 3 + d], along((y + d) % NY, h),
         )
 
-    loads[1].wait()
+    for load in loads[1:5]:
+        load.wait()
     pick(0)
 
     @pl.when(jnp.logical_not(is_src))
@@ -289,13 +292,23 @@
             pick(ch)
         for d in (2, 1, 3):
             one(d, ch).start()
+        if ch == 0:
+            @pl.when(first_plane & (x > 0) & (r == 0))
+            def _():
+                arrived(x, FIX)
+                for step in (1, 2, 4, 6):
+                    down(step).start()
 
     def goes_x(leap, t):
-        if leap == 1:
-            return (z > 0) | (x == 1) | ((x == 2) & (t < 2))
-        if leap == 3:
-            return (z > 0) | (x == 2) | (x == 3)
-        return z > 0
+        return (z > 0) | (((x + leap) % NX != 0) & ((x != 2) | (leap != 1) | (t < 2)))
+
+    def along_x(t, carry):
+        for leap in (1, 3, 2):
+            @pl.when(goes_x(leap, t))
+            def _():
+                net(x, t, 5 * leap + t, chip((x + leap) % NX, z)).start()
+
+        return carry
 
     def own(t, carry):
         arrived(x, t)
@@ -309,10 +322,9 @@
         def _():
             net(x, t, t, chip(x, z + 1)).start()
 
-        for leap in (2, 1, 3):
-            @pl.when(goes_x(leap, t))
-            def _():
-                net(x, t, 5 * leap + t, chip((x + leap) % NX, z)).start()
+        @pl.when(z > 0)
+        def _():
+            along_x(t, 0)
 
         return carry
 
@@ -335,9 +347,6 @@
 
         for leap in (2, 1, 3):
             net(x, FIX, 5 * leap + FIX, chip((x + leap) % NX, z)).start()
-
-    def goes_back(q):
-        return (z == 1) & (((x > 0) & (q == 0)) | ((x == 1) & (q == 3)) | ((x == 3) & (q == 1)))
 
     def relayed(q, t):
         return first_plane & (x == 3) & (q == 2) & (t >= 2)
@@ -350,26 +359,16 @@
             def _():
                 arrived(q, t)
 
-            @pl.when(goes_back(q))
-            def _():
-                net(q, t, 15 + 5 * leap + t, chip(x, 0)).start()
-
         return carry
 
     def other_lines(low, high):
         lax.fori_loop(low, high, others, 0)
 
-    @pl.when(first_plane & (x > 0) & (r == 0))
-    def _():
-        arrived(x, FIX)
-        for step in (1, 2, 4, 6):
-            down(step).start()
-
-    own_line(0, jnp.where(z == 0, 4, jnp.where(z == 1, 1, 0)))
-
-    @pl.when(first_plane & (r > 0))
-    def _():
-        own_fix_line()
+    early = (r == 1) | ((h == 0) & (r > 0))
+    late = (h == 1) & (r > 1)
+    own_line(0, jnp.where(z == 0, jnp.where(early, 2, 4), jnp.where(z == 1, 1, 0)))
+    pl.when(first_plane & early)(own_fix_line)
+    own_line(jnp.where(first_plane & early, 2, 4), 4)
 
     home = pl.ds(pl.multiple_of(y * part, part), part)
     home_owner = wide(owner_of(pl.multiple_of(y * part, part), part), width)
@@ -394,7 +393,7 @@
         zs[:, columns(ch)] = sent_rows.astype(jnp.bfloat16)
         two(ch).start()
 
-    for load in loads[2:]:
+    for load in loads[5:]:
         load.wait()
 
     def inverses():
@@ -402,19 +401,16 @@
         lb = balanced(linv[...].astype(jnp.float32)).astype(jnp.bfloat16)
         both[...] = balanced(dot(ub, lb)).astype(jnp.bfloat16)
 
-    pl.when(z != 1)(inverses)
-
-    own_line(
-        jnp.where(z == 0, 4, jnp.where(z == 1, 1, 0)),
-        jnp.where(z < 3, 4, 2),
-    )
-
-    @pl.when(z == 1)
-    def _():
-        pl.when(r > 0)(own_fix_line)
-        other_lines(0, 2)
-        core_line(0).start()
-        core_line(1).start()
+    pl.when(first_plane & late)(own_fix_line)
+
+    @pl.when(first_plane & (x > 0))
+    def _():
+        lax.fori_loop(0, 4, along_x, 0)
+
+    inverses()
+    own_line(jnp.where(z == 0, 4, jnp.where(z == 1, 1, 0)), jnp.where(z < 2, 4, 4 - z))
+    pl.when((z > 0) & (r > 0))(own_fix_line)
+    own_line(jnp.where(z < 2, 4, 4 - z), jnp.where(z < 2, 4, 2))
 
     for ch in range(CHUNKS):
         two(ch).wait_recv()
@@ -432,18 +428,7 @@
             three(d, ch).start()
         xf[home, columns(ch)] = jnp.where(home_owner == r, old, new).astype(jnp.bfloat16)
 
-    own_line(jnp.where(z < 3, 4, 2), 4)
-
-    @pl.when((z >= 2) & (r > 0))
-    def _():
-        own_fix_line()
-
-    @pl.when(z == 1)
-    def _():
-        other_lines(2, 4)
-        core_line(2).start()
-        core_line(3).start()
-        inverses()
+    own_line(jnp.where(z < 2, 4, 2), 4)
 
     @pl.when(r > 0)
     def _():
@@ -510,7 +495,7 @@
         own_copy.wait()
 
     for i in range(2):
-        @pl.when((z != 1) & jnp.logical_not(is_src))
+        @pl.when(jnp.logical_not(is_src))
         def _():
             other_lines(2 * i, 2 * i + 2)
             core_line(2 * i).start()
@@ -570,11 +555,6 @@
     for leap in range(1, 4):
         pl.when(r > 0)(lambda: sent(5 * leap + FIX))
 
-        @pl.when(goes_back((x + leap) % NX))
-        def _():
-            for t in range(4):
-                sent(15 + 5 * leap + t)
-
     @pl.when(first_plane & (x == 3))
     def _():
         sent(38)
@@ -588,7 +568,7 @@
         @pl.when(r == 0)
         def _():
             for q in (2, 1, 3):
-                fix_out(q, 25 + q).wait_send()
+                fix_out(q, 36 + q).wait_send()
 
         @pl.when(k == 0)
         def _():
@@ -640,8 +620,8 @@
             pltpu.VMEM((part, cols), bf),
             pltpu.VMEM((part, cols), bf),
             pltpu.VMEM((NY - 1, part, cols), bf),
-            dma((42,)), dma((20,)), dma((29,)), dma((5,)), dma((5,)), dma((5,)),
-            dma((7,)), dma((7 * CHUNKS,)), dma((7 * CHUNKS,)), dma((6,)), dma((4,)),
+            dma((42,)), dma((20,)), dma((40,)), dma((5,)), dma((5,)), dma((5,)),
+            dma((7,)), dma((7 * CHUNKS,)), dma((7 * CHUNKS,)), dma((9,)), dma((4,)),
         ],
         compiler_params=pltpu.CompilerParams(
             collective_id=0, has_side_effects=True, vmem_limit_bytes=60 << 20
@@ -650,11 +630,45 @@
     )(piv, linv, uinv, s)
 
 
+def divide_kernel(x_hbm, o_hbm, x, o, sem_in, sem_out):
+    parts = sem_in.shape[0]
+    size = x.shape[0] // parts
+    spans = [pl.ds(i * size, size) for i in range(parts)]
+    loads = [pltpu.make_async_copy(x_hbm.at[at], x.at[at], sem_in.at[i]) for i, at in enumerate(spans)]
+    stores = [pltpu.make_async_copy(o.at[at], o_hbm.at[at], sem_out.at[i]) for i, at in enumerate(spans)]
+    for load in loads:
+        load.start()
+    for at, load, store in zip(spans, loads, stores):
+        load.wait()
+        o[at, :] = x[at, :].astype(jnp.float32) * INVERSE
+        store.start()
+    for store in stores:
+        store.wait()
+
+
+def divide(x):
+    anywhere = pl.BlockSpec(memory_space=pl.ANY)
+    parts = 8
+    return pl.pallas_call(
+        divide_kernel,
+        out_shape=jax.ShapeDtypeStruct(x.shape, jnp.float32),
+        in_specs=[anywhere],
+        out_specs=anywhere,
+        scratch_shapes=[
+            pltpu.VMEM(x.shape, x.dtype),
+            pltpu.VMEM(x.shape, jnp.float32),
+            pltpu.SemaphoreType.DMA((parts,)),
+            pltpu.SemaphoreType.DMA((parts,)),
+        ],
+        compiler_params=pltpu.CompilerParams(vmem_limit_bytes=60 << 20),
+        name="divide",
+    )(x)
+
+
 def per_device(matrix, pivots, lower_inverse, upper_inverse):
     panel = lower_inverse.shape[0]
     piv = pivots.reshape(1, panel)
-    rest = step_kernel(piv, lower_inverse, upper_inverse, matrix, panel)
-    return rest.astype(jnp.float32) * INVERSE
+    return divide(step_kernel(piv, lower_inverse, upper_inverse, matrix, panel))
 
 
 def solution(mesh):

time: 60.6 us -> 54.2 us (0.89)
  the two profiles are of different devices: /device:TPU:105 before, /device:TPU:41 now
where the time goes in v3:
time: 54.2 us; the launch traced here: 53.3 us
  Pallas kernels  53.3 us (98%)
    pallas_call x1, Pallas kernels, step_kernel(): pl.pallas_call(exchange_kernel, out_shape=jax.ShapeDtypeStruct((rows, col...  50.2 us
    pallas_call x1, Pallas kernels, divide(): pl.pallas_call(divide_kernel, out_shape=jax.ShapeDtypeStruct(x.shape, jnp...  3.13 us

profile of v3, /device:TPU:41, one launch (start us, length us, event | category | flops | bytes accessed | tf_op | source)
XLA Modules:
  0.0 53.3 jit_solution(9603706274120679732)
XLA Ops:
  0.0 50.2 %exchange.1.x_hbm = bf16[2048,512]{1,0:T(8,128)(2,1)} custom-call(s32[1,512]{1,0:T(1,128)} %bitcast.1, bf16[512,512]{1,0:T(8,128)(2,1)} %linv_hbm.1, bf16[512,512]{1,0:T(8,128)(2,1)} %uinv_hbm.1, bf16[2048,512]{1,0:T(8,128)(2,1)} %s_hbm.1), custom_call_target="tpu_custom_call" | custom-call | tf_op jit(solution)/shard_map/exchange/pallas_call | solution.py:599
  50.2 3.1 %divide.1 = f32[2048,512]{1,0:T(8,128)} custom-call(bf16[2048,512]{1,0:T(8,128)(2,1)} %exchange.1.x_hbm), custom_call_target="tpu_custom_call" | custom-call | tf_op jit(solution)/shard_map/divide/pallas_call | solution.py:652

commit v4 on v3

--- a/solution.py
+++ b/solution.py
@@ -366,9 +366,9 @@
 
     early = (r == 1) | ((h == 0) & (r > 0))
     late = (h == 1) & (r > 1)
-    own_line(0, jnp.where(z == 0, jnp.where(early, 2, 4), jnp.where(z == 1, 1, 0)))
+    own_line(0, jnp.where(z == 0, jnp.where(early, 2, jnp.where(x == 1, 3, 4)), jnp.where(z == 1, 1, 0)))
     pl.when(first_plane & early)(own_fix_line)
-    own_line(jnp.where(first_plane & early, 2, 4), 4)
+    own_line(jnp.where(first_plane & early, 2, 4), jnp.where(first_plane & (x == 1), 3, 4))
 
     home = pl.ds(pl.multiple_of(y * part, part), part)
     home_owner = wide(owner_of(pl.multiple_of(y * part, part), part), width)
@@ -401,15 +401,15 @@
         lb = balanced(linv[...].astype(jnp.float32)).astype(jnp.bfloat16)
         both[...] = balanced(dot(ub, lb)).astype(jnp.bfloat16)
 
+    own_line(jnp.where(first_plane & (x == 1), 3, 4), 4)
     pl.when(first_plane & late)(own_fix_line)
 
     @pl.when(first_plane & (x > 0))
     def _():
         lax.fori_loop(0, 4, along_x, 0)
 
-    inverses()
     own_line(jnp.where(z == 0, 4, jnp.where(z == 1, 1, 0)), jnp.where(z < 2, 4, 4 - z))
-    pl.when((z > 0) & (r > 0))(own_fix_line)
+    pl.when((z == 3) & (r > 0))(own_fix_line)
     own_line(jnp.where(z < 2, 4, 4 - z), jnp.where(z < 2, 4, 2))
 
     for ch in range(CHUNKS):
@@ -428,7 +428,9 @@
             three(d, ch).start()
         xf[home, columns(ch)] = jnp.where(home_owner == r, old, new).astype(jnp.bfloat16)
 
+    pl.when((z > 0) & (z < 3) & (r > 0))(own_fix_line)
     own_line(jnp.where(z < 2, 4, 2), 4)
+    inverses()
 
     @pl.when(r > 0)
     def _():

time: 54.2 us -> 53.5 us (0.987); the launches traced: 53.3 us -> 53.3 us
  no operation moved by 1% of the time
where the time goes in v4:
time: 53.5 us; the launch traced here: 53.3 us
  Pallas kernels  53.3 us (100%)
    pallas_call x1, Pallas kernels, step_kernel(): pl.pallas_call(exchange_kernel, out_shape=jax.ShapeDtypeStruct((rows, col...  50.2 us
    pallas_call x1, Pallas kernels, divide(): pl.pallas_call(divide_kernel, out_shape=jax.ShapeDtypeStruct(x.shape, jnp...  3.13 us

profile of v4, /device:TPU:41, one launch (start us, length us, event | category | flops | bytes accessed | tf_op | source)
XLA Modules:
  0.0 53.3 jit_solution(18008008845268927408)
XLA Ops:
  0.0 50.2 %exchange.1.x_hbm = bf16[2048,512]{1,0:T(8,128)(2,1)} custom-call(s32[1,512]{1,0:T(1,128)} %bitcast.1, bf16[512,512]{1,0:T(8,128)(2,1)} %linv_hbm.1, bf16[512,512]{1,0:T(8,128)(2,1)} %uinv_hbm.1, bf16[2048,512]{1,0:T(8,128)(2,1)} %s_hbm.1), custom_call_target="tpu_custom_call" | custom-call | tf_op jit(solution)/shard_map/exchange/pallas_call | solution.py:601
  50.2 3.1 %divide.1 = f32[2048,512]{1,0:T(8,128)} custom-call(bf16[2048,512]{1,0:T(8,128)(2,1)} %exchange.1.x_hbm), custom_call_target="tpu_custom_call" | custom-call | tf_op jit(solution)/shard_map/divide/pallas_call | solution.py:654

commit v5 on v4

--- a/solution.py
+++ b/solution.py
@@ -31,7 +31,7 @@
 
 
 def exchange_kernel(
-    piv_hbm, linv_hbm, uinv_hbm, s_hbm, o_hbm, piv_ref, linv, uinv, out, pf, tt, xf, both, wk, rep, s_ref, pcol, oh, g, r1, zs, r2, msg,
+    piv_hbm, linv_hbm, uinv_hbm, s_hbm, o_hbm, piv_ref, linv, uinv, out, hits, pf, tt, xf, both, wk, rep, s_ref, pcol, oh, g, r1, zs, r2, msg,
     net_send, net_recv, src_send, src_recv, core_send, core_recv, down_send, row_send, row_recv, loc, out_sem,
 ):
     rows = s_ref.shape[0]
@@ -432,6 +432,14 @@
     own_line(jnp.where(z < 2, 4, 2), 4)
     inverses()
 
+    def mark(t, carry):
+        start = pl.multiple_of(t * 128, 128)
+        index = lax.broadcasted_iota(jnp.int32, (128, panel), 0) + (r * rows + start)
+        hits[pl.ds(start, 128), :] = jnp.where(index == piv_ref[...], 1.0, 0.0).astype(jnp.bfloat16)
+        return carry
+
+    lax.fori_loop(0, rows // 128, mark, 0)
+
     @pl.when(r > 0)
     def _():
         for leap in (2, 1, 3):
@@ -483,9 +491,7 @@
 
         @pl.when((r > 0) | (start >= panel))
         def _():
-            index = lax.broadcasted_iota(jnp.int32, (panel, panel), 0) + (r * rows + start)
-            hit = jnp.where(index == piv_ref[...], 1.0, 0.0).astype(bf)
-            swapped = dot(hit, rep[...])
+            swapped = dot(hits[at, :], rep[...])
             count = wide(swapped[:, panel : panel + 128], panel)
             rest = residue(s_ref[at, :].astype(jnp.float32) * keep + dot(pf[at, :], wk[...]))
             out[at, :] = jnp.where(count > 0, swapped[:, 0:panel], rest).astype(bf)
@@ -608,6 +614,7 @@
             pltpu.VMEM((panel, panel), bf),
             pltpu.VMEM((panel, panel), bf),
             pltpu.VMEM((rows, cols), bf),
+            pltpu.VMEM((rows, panel), bf),
             pltpu.VMEM((rows + panel, panel), bf),
             pltpu.VMEM((panel, cols), bf),
             pltpu.VMEM((panel, cols), bf),

time: 53.5 us -> 53.5 us (level)
  no operation moved by 1% of the time
where the time goes in v5:
time: 53.5 us; the launch traced here: 53.3 us
  Pallas kernels  53.3 us (100%)
    pallas_call x1, Pallas kernels, step_kernel(): pl.pallas_call(exchange_kernel, out_shape=jax.ShapeDtypeStruct((rows, col...  50.2 us
    pallas_call x1, Pallas kernels, divide(): pl.pallas_call(divide_kernel, out_shape=jax.ShapeDtypeStruct(x.shape, jnp...  3.13 us

profile of v5, /device:TPU:41, one launch (start us, length us, event | category | flops | bytes accessed | tf_op | source)
XLA Modules:
  0.0 53.3 jit_solution(3430262767192811463)
XLA Ops:
  0.0 50.2 %exchange.1.x_hbm = bf16[2048,512]{1,0:T(8,128)(2,1)} custom-call(s32[1,512]{1,0:T(1,128)} %bitcast.1, bf16[512,512]{1,0:T(8,128)(2,1)} %linv_hbm.1, bf16[512,512]{1,0:T(8,128)(2,1)} %uinv_hbm.1, bf16[2048,512]{1,0:T(8,128)(2,1)} %s_hbm.1), custom_call_target="tpu_custom_call" | custom-call | tf_op jit(solution)/shard_map/exchange/pallas_call | solution.py:607
  50.2 3.1 %divide.1 = f32[2048,512]{1,0:T(8,128)} custom-call(bf16[2048,512]{1,0:T(8,128)(2,1)} %exchange.1.x_hbm), custom_call_target="tpu_custom_call" | custom-call | tf_op jit(solution)/shard_map/divide/pallas_call | solution.py:661
